TPU v7x, 32 devices: a whole 2x2x4 slice. The times are simulated.
32 devices in a mesh: groups: 2 (over x), blk: 4 (over y, core), row: 4 (over z).
Axes of the slice: x: 2, y: 2, z: 4, core: 2. Of those that a mesh axis runs over, the one named last changes fastest.
Arguments:
- coords: float32 [3, 24576], P(None, ('groups', 'blk', 'row')), parts along dimension 1, may hold values from 0 to 1
- charges: float32 [24576], P(('groups', 'blk', 'row')), parts along dimension 0, may hold values from -1 to 1
- counts: int32 [32], P(('groups', 'blk', 'row')), parts along dimension 0, may hold values from 256 to 768, as said below
- send_slot: int32 [24576], P(('groups', 'blk', 'row')), parts along dimension 0, may hold values from 0 to 1023, as said below
- recv_index: int32 [16384], P(('groups', 'blk', 'row')), parts along dimension 0, may hold values from 0 to 1023, as said below
- wave_ints: int32 [3, 24576], P(None, 'blk'), may hold values from -36 to 36, as said below
Outputs:
- slot_forces: float32 [3, 24576], P(None, ('groups', 'blk', 'row')), parts along dimension 1
- atom_forces: float32 [3, 16384], P(None, ('groups', 'blk', 'row')), parts along dimension 1
There are 2 independent parts, one for each index of `groups`. A program takes and returns all parts, laid end to end along the dimension named above; an argument that names none is the same for every part. Nothing has to cross between parts.
Inputs may be any that keep to these rules, and one draw needn't show every extreme that they name: The counts of one system sum to 8192; the largest is 768. `send_slot`: for a live slot the value is d * 64 + r: the ion goes to k-space device d as its r-th arrival from this owner. Live values of one owner are distinct, and the ranks r to one device are 0 up to the number sent there minus one. Every device receives exactly 512 ions; some owner sends exactly 64 to some device. Slots that are not live hold arbitrary values. `recv_index`: the 512 values of device d are distinct and are exactly the arrivals s * 64 + r sent to d. `wave_ints`: each column is (h, k, l) with |h|, |k| at most 12 and l nonzero.
All inputs are finite; a program needn't handle non-finite values.
Results may differ from a plain program's by a relative error of at most 0.00007.
Values sent between devices are 32-bit elements; how exact they have to be, the bound alone decides.
A program may use at most 128 MiB of HBM per device.

v0:
```python
import math

import jax
import jax.numpy as jnp
from jax import lax
from jax.sharding import PartitionSpec as P

DOUBLE_PI = 2.0 * math.pi
EWALD_BETA = 30.0
BOX_Z = 3.0
FORCE_GAIN = 400.0


def phys_vectors(wave_float):
    return jnp.stack(
        [DOUBLE_PI * wave_float[0], DOUBLE_PI * wave_float[1], DOUBLE_PI * wave_float[2] / BOX_Z]
    )


def phase_angles(wave_float, frac):
    inner = wave_float[0][:, None] * frac[0][None, :] + wave_float[1][:, None] * frac[1][None, :]
    inner = inner + wave_float[2][:, None] * frac[2][None, :]
    return DOUBLE_PI * inner


def pull_sum(wave_float, cos_weighted, sin_weighted, frac):
    angles = phase_angles(wave_float, frac)
    coef = jnp.sin(angles) * cos_weighted[:, None] - jnp.cos(angles) * sin_weighted[:, None]
    wave_phys = phys_vectors(wave_float)
    return jnp.sum(wave_phys[:, :, None] * coef[None, :, :], axis=1)


def phase_sums(wave_float, atom_rows):
    angles = phase_angles(wave_float, atom_rows[:3])
    return (
        jnp.sum(atom_rows[3][None, :] * jnp.cos(angles), axis=1),
        jnp.sum(atom_rows[3][None, :] * jnp.sin(angles), axis=1),
    )


def body(coords, charges, counts, send_slot, recv_index, wave_ints):
    slots_dev = charges.shape[0]
    atoms_dev = recv_index.shape[0]
    devices = lax.axis_size(("blk", "row"))
    blk_count = lax.axis_size("blk")
    pair_cap = 2 * atoms_dev // devices
    buf_width = devices * pair_cap
    is_live = jnp.arange(slots_dev, dtype=jnp.int32) < counts[0]
    target_slot = jnp.where(is_live, send_slot, buf_width)
    value_entries = jnp.concatenate([coords, charges[None, :]], axis=0)
    outgoing = (
        jnp.zeros((4, buf_width), jnp.float32).at[:, target_slot].set(value_entries, mode="drop")
    )
    arrived = lax.all_to_all(
        outgoing.reshape(4, devices, pair_cap),
        ("blk", "row"),
        split_axis=1,
        concat_axis=1,
        tiled=True,
    )
    atom_rows = arrived.reshape(4, buf_width)[:, recv_index]
    k_local = wave_ints.shape[1]
    wave_float = wave_ints.astype(jnp.float32)
    cos_part, sin_part = phase_sums(
        wave_float, lax.all_gather(atom_rows, "blk", axis=1, tiled=True)
    )
    cos_sum, sin_sum = lax.psum((cos_part, sin_part), "row")
    wave_phys = phys_vectors(wave_float)
    k_squared = jnp.sum(wave_phys * wave_phys, axis=0)
    weight = jnp.exp(-k_squared / (4.0 * EWALD_BETA * EWALD_BETA)) / k_squared
    cos_weighted = weight * cos_sum
    sin_weighted = weight * sin_sum
    force_scale = FORCE_GAIN / math.sqrt(float(atoms_dev * devices * blk_count * k_local))
    package = jnp.concatenate([wave_float, cos_weighted[None, :], sin_weighted[None, :]], axis=0)
    shard_piece = lax.all_gather(package, "blk", axis=1, tiled=True)
    pull_total = pull_sum(shard_piece[:3], shard_piece[3], shard_piece[4], atom_rows[:3])
    atom_forces = force_scale * atom_rows[3][None, :] * pull_total
    homeward = jnp.zeros((3, buf_width), jnp.float32).at[:, recv_index].set(atom_forces)
    returned = lax.all_to_all(
        homeward.reshape(3, devices, pair_cap),
        ("blk", "row"),
        split_axis=1,
        concat_axis=1,
        tiled=True,
    ).reshape(3, buf_width)
    picked = returned[:, jnp.minimum(target_slot, buf_width - 1)]
    slot_forces = jnp.where(is_live[None, :], picked, 0.0)
    return (slot_forces, atom_forces)


def solution(mesh):
    placed = (
        P(None, ("groups", "blk", "row")),
        P(("groups", "blk", "row")),
        P(("groups", "blk", "row")),
        P(("groups", "blk", "row")),
        P(("groups", "blk", "row")),
        P(None, "blk"),
    )
    return jax.shard_map(
        body,
        mesh=mesh,
        in_specs=placed,
        out_specs=(P(None, ("groups", "blk", "row")), P(None, ("groups", "blk", "row"))),
        check_vma=False,
    )
```

profile of v0, /device:TPU:1, one launch (start us, length us, event | category | flops | bytes accessed | tf_op | source)
XLA Modules:
  0.0 503.1 jit_solution(13282981945694816931)
XLA Ops:
  1.3 0.7 broadcast_in_dim.50
  2.0 0.7 maximum_bitcast_fusion
  2.7 0.2 copy.21
  2.9 0.7 compare_select_fusion
  3.6 4.3 scatter_custom_fusion
  7.9 0.2 copy.22
  8.1 0.7 reshape.201
  8.8 7.4 %all-to-all-start = ((f32[16,1,256]{2,1,0:T(1,128)}), f32[16,1,256]{2,1,0:T(1,128)S(1)}, u32[]{:S(2)}, u32[]{:S(2)}) async-start(f32[16,1,256]{2,1,0:T(1,128)} %reshape.201), calls=%async_computation | async-start | bytes 32768 | tf_op jit(solution)/shard_map/all_to_all | solution.py:54
  16.1 0.7 compare_select_fusion.2
  16.8 0.9 convert_element_type.3
  17.8 0.1 broadcast_multiply_fusion.5
  17.9 0.1 fusion.5
  18.0 4.3 all-to-all-done
  22.3 0.5 broadcast.143
  22.8 0.7 reduce.16
  23.5 0.1 reshape.202
  23.6 0.2 copy.23
  23.8 1.0 gather_fusion
  24.9 10.1 %all-gather = f32[4,2048]{0,1:T(8,128)S(1)} all-gather(f32[4,512]{0,1:T(8,128)S(1)} %bitcast.28), channel_id=2, replica_groups=mesh['groups'=2,'blk'=4,'row'=4] {'blk'}, dimensions={1}, use_global_device_ids=true | all-gather | bytes 40960 | tf_op jit(solution)/shard_map/all_gather | solution.py:65
  35.0 0.6 fusion
  35.6 2.0 slice_reduce_fusion.3
  37.6 213.6 %multiply_reduce_fusion.2 = (f32[6144]{0:T(1024)S(1)}, f32[6144]{0:T(1024)S(1)}) fusion(f32[2048]{0:T(1024)S(1)} %get-tuple-element.13, f32[6144]{0:T(1024)S(1)} %bitcast.45, f32[2048]{0:T(1024)S(1)} %get-tuple-element.11, f32[6144]{0:T(1024)S(1)} %bitcast.46, f32[2048]{0:T(1024)S(1)} %get-tuple-element.12, f32[6144]{0:T(1024)S(1)} %bitcast.47, ...), kind=kLoop, calls=%fused_computation.7 | loop fusion | flops 125816832 | bytes 155648 | tf_op jit(solution)/shard_map/reduce_sum | solution.py:36
  251.2 13.0 %all-reduce = (f32[6144]{0:T(1024)S(1)}, f32[6144]{0:T(1024)S(1)}) all-reduce(f32[6144]{0:T(1024)S(1)} %get-tuple-element.19, f32[6144]{0:T(1024)S(1)} %get-tuple-element.18), channel_id=1, replica_groups=mesh['groups'=2,'blk'=4,'row'=4] {'row'}, use_global_device_ids=true, to_apply=%region_5.6 | all-reduce | flops 12288 | bytes 98304 | tf_op jit(solution)/shard_map/psum | solution.py:67
  264.2 0.1 pad_maximum_fusion.1
  264.3 11.4 %all_gather.7 = f32[5,24576]{1,0:T(8,128)S(1)} all-gather(f32[5,6144]{1,0:T(8,128)S(1)} %pad_maximum_fusion.1), channel_id=1, replica_groups=mesh['groups'=2,'blk'=4,'row'=4] {'blk'}, dimensions={1}, use_global_device_ids=true | all-gather | bytes 614400 | tf_op jit(solution)/shard_map/all_gather | solution.py:75
  275.7 0.5 broadcast_multiply_fusion.2
  276.3 0.3 pad_maximum_fusion
  276.5 192.7 %multiply_subtract_fusion = f32[24576,512]{1,0:T(8,128)} fusion(f32[24576]{0:T(1024)S(1)} %bitcast.34, f32[24576]{0:T(1024)S(1)} %bitcast.35, f32[512]{0:T(512)S(1)} %get-tuple-element.16, f32[24576]{0:T(1024)S(1)} %bitcast.36, f32[512]{0:T(512)S(1)} %get-tuple-element.17, f32[24576]{0:T(1024)S(1)} %bitcast.37, f32[512]{0:T(512)S(1)} %get-tuple-element.15, ...), kind=kLoop, calls=%fused_computation.5 | loop fusion | flops 113246208 | bytes 50829312 | tf_op jit(solution)/shard_map/sub | solution.py:28
  469.3 17.6 %multiply_reduce_fusion = f32[3,512]{1,0:T(4,128)S(1)} fusion(f32[24576,512]{1,0:T(8,128)} %multiply_subtract_fusion, f32[3,24576]{1,0:T(4,128)S(1)} %pad_maximum_fusion), kind=kLoop, calls=%fused_computation.4 | loop fusion | flops 75495936 | bytes 50632704 | tf_op jit(solution)/shard_map/reduce_sum | solution.py:30
  486.8 0.1 copy.24
  487.0 1.8 scatter_custom_fusion.1
  488.8 0.2 copy.25
  489.1 0.7 reshape.203
  489.8 3.7 all-to-all-start.1
  493.4 0.6 broadcast_multiply_fusion.6
  494.0 5.5 %all-to-all-done.1 = f32[16,1,192]{2,1,0:T(1,128)S(1)} async-done(((f32[16,1,192]{2,1,0:T(1,128)}), f32[16,1,192]{2,1,0:T(1,128)S(1)}, u32[]{:S(2)}, u32[]{:S(2)}) %all-to-all-start.1) | async-done | bytes 12320 | tf_op jit(solution)/shard_map/all_to_all | solution.py:79
  499.6 0.7 reduce.17
  500.3 0.1 reshape.204
  500.3 0.2 copy.26
  500.6 1.6 gather_fusion.1
  502.2 0.2 select_bitcast_fusion
  502.4 0.8 copy.27
  (5 shorter events, 0.0 us)
Async XLA Ops:
  8.8 13.5 %all-to-all-start = ((f32[16,1,256]{2,1,0:T(1,128)}), f32[16,1,256]{2,1,0:T(1,128)S(1)}, u32[]{:S(2)}, u32[]{:S(2)}) async-start(f32[16,1,256]{2,1,0:T(1,128)} %reshape.201), calls=%async_computation | async-start | bytes 32768 | tf_op jit(solution)/shard_map/all_to_all | solution.py:54
  489.8 9.8 %all-to-all-start.1 = ((f32[16,1,192]{2,1,0:T(1,128)}), f32[16,1,192]{2,1,0:T(1,128)S(1)}, u32[]{:S(2)}, u32[]{:S(2)}) async-start(f32[16,1,192]{2,1,0:T(1,128)} %reshape.203), calls=%async_computation.1 | async-start | bytes 32768 | tf_op jit(solution)/shard_map/all_to_all | solution.py:79
where the time goes:
time: 504 us; the launch traced here: 503 us
  other arithmetic  431 us (86%)
  blocking collectives  34.6 us (7%)
  local copies, waits for them, and re-layouts  15.5 us (3%)
  starting transfers between devices  11 us (2%)
  waiting for transfers between devices  9.79 us (2%)
    reduce_sum x1, other arithmetic, phase_sums(): jnp.sum(atom_rows[3][None, :] * jnp.cos(angles), axis=1)  214 us
    sub x1, other arithmetic, pull_sum(): jnp.sin(angles) * cos_weighted[:, None]  193 us
    reduce_sum x1, other arithmetic, pull_sum(): return jnp.sum(wave_phys[:, :, None] * coef[None, :, :], axis=1)  17.6 us
    psum x1, blocking collectives, body(): cos_sum, sin_sum = lax.psum((cos_part, sin_part), 'row')  13 us
    all_gather x1, blocking collectives, body(): shard_piece = lax.all_gather(package, 'blk', axis=1, tiled=True)  11.4 us
    all_gather x1, blocking collectives, body(): lax.all_gather(atom_rows, 'blk', axis=1, tiled=True)  10.1 us
  transfers between devices with their start and end apart: 2, of which 2 were waited for; matrix products, arithmetic and copies ran while one was open for 0% of the time, Pallas kernels for 0%

commit v1 on v0

v1 whole, which is shorter than its diff:
```python
import functools
import math

import jax
import jax.numpy as jnp
from jax import lax
from jax.experimental import pallas as pl
from jax.experimental.pallas import tpu as pltpu
from jax.sharding import PartitionSpec as P

EWALD_BETA = 30.0
BOX_Z = 3.0
FORCE_GAIN = 400.0
HMAX = 12
LMAX = 36
SIDE = 2 * HMAX
FOLD = (2 * HMAX + 1) * SIDE
PAIRS = 640
L_ROWS = 2 * LMAX
L_TILES = L_ROWS // 8
P_TILES = PAIRS // 128
TILES = L_TILES * P_TILES
F32 = jnp.float32
BF16 = jnp.bfloat16

SIN_C = [(-1) ** n * math.pi ** (2 * n + 1) / math.factorial(2 * n + 1) for n in range(7)]
COS_C = [(-1) ** n * math.pi ** (2 * n) / math.factorial(2 * n) for n in range(8)]
NT = (((1,), (1,)), ((), ()))
NN = (((1,), (0,)), ((), ()))


def iota(shape, dim):
    return lax.broadcasted_iota(jnp.int32, shape, dim)


def horner(coefs, u):
    out = jnp.full_like(u, coefs[-1])
    for c in coefs[-2::-1]:
        out = out * u + c
    return out


def turns(mult, frac):
    high = jnp.floor(frac * 4096.0 + 0.5) * (1.0 / 4096.0)
    low = frac - high
    whole = mult * high
    r = (whole - jnp.floor(whole + 0.5)) + mult * low
    u = r * r
    s = r * horner(SIN_C, u)
    c = horner(COS_C, u)
    return 1.0 - 2.0 * s * s, 2.0 * s * c


def split2(x):
    hi = x.astype(BF16)
    return hi, (x - hi.astype(F32)).astype(BF16)


def split3(x):
    hi = x.astype(BF16)
    rest = x - hi.astype(F32)
    mid = rest.astype(BF16)
    return hi, mid, (rest - mid.astype(F32)).astype(BF16)


def mm(a, b, dims):
    return lax.dot_general(a, b, dims, preferred_element_type=F32)


def l_column():
    row = iota((L_ROWS, 1), 0)
    return (4 * (row // 8) + row % 4 + 1).astype(F32), (row % 8) < 4


def pair_rows():
    n = iota((1, PAIRS), 1)
    tall = n < FOLD
    q = n // SIDE
    h = jnp.where(tall, q - HMAX, n - FOLD - HMAX)
    k = jnp.where(tall, n - q * SIDE - HMAX, HMAX)
    return h.astype(F32), k.astype(F32)


def fill_pairs(frac_x, frac_y, tables):
    width = frac_x.shape[1]
    mult = (iota((32, 1), 0) - HMAX).astype(F32)
    cx, sx = turns(mult, frac_x)
    cy, sy = turns(mult, frac_y)
    cyk, syk = cy[:SIDE], sy[:SIDE]

    def put(start, c, s):
        rows = pl.ds(start, c.shape[0])
        for value, (hi_ref, lo_ref) in ((c, tables[:2]), (s, tables[2:])):
            hi, lo = split2(value)
            hi_ref[rows, :] = hi
            lo_ref[rows, :] = lo

    def one(i):
        a, b = cx[i : i + 1], sx[i : i + 1]
        return a * cyk - b * syk, b * cyk + a * syk

    for i in range(0, 2 * HMAX, 2):
        (c0, s0), (c1, s1) = one(i), one(i + 1)
        put(i * SIDE, jnp.concatenate([c0, c1]), jnp.concatenate([s0, s1]))
    c0, s0 = one(2 * HMAX)
    a, b = cy[SIDE : SIDE + 1], sy[SIDE : SIDE + 1]
    pad = jnp.zeros((8, width), F32)
    put(
        2 * HMAX * SIDE,
        jnp.concatenate([c0, cx * a - sx * b, pad]),
        jnp.concatenate([s0, sx * a + cx * b, pad]),
    )


def tiles_out(ref, value, count):
    for t in range(count):
        if t < TILES:
            i, j = t // P_TILES, t % P_TILES
            ref[t] = value[8 * i : 8 * i + 8, 128 * j : 128 * j + 128]
        else:
            ref[t] = jnp.zeros((8, 128), F32)


def local_kernel(
    devices, rows, cap, tile_count,
    coords, charges, counts, send_slot, wave,
    sums, mult, posts, *tables,
):
    slots = coords.shape[1]
    me = lax.axis_index("blk") * rows + lax.axis_index("row")
    live = iota((1, slots), 1) < counts[...]
    q = jnp.where(live, charges[...], 0.0)
    target = jnp.where(live, send_slot[...], -1)
    width = devices * cap
    spots = jnp.where(target == iota((width, slots), 0), 1.0, 0.0).astype(BF16)
    entries = jnp.concatenate([coords[...], q, jnp.zeros((4, slots), F32)])
    out = sum(mm(term, spots, NT) for term in split3(entries))
    per_tile = 128 // cap
    lane_part = iota((8, 128), 1) // cap
    for d in range(devices):
        tile = out[:, 128 * (d // per_tile) : 128 * (d // per_tile) + 128]
        tile = jnp.where(lane_part == d % per_tile, tile, 0.0)
        shift = (me % per_tile - d % per_tile + per_tile) % per_tile * cap
        posts[d] = pltpu.roll(tile, shift, 1)
    k_local = wave.shape[1]
    part = k_local // rows
    split = part % 128 == 0 and part * rows == k_local
    if split:
        w = wave[:, pl.ds(pl.multiple_of(lax.axis_index("row") * part, 128), part)]
    else:
        w = wave[...]
    h, k, l = w[0:1], w[1:2], w[2:3]
    sign = jnp.where(l < 0, -1, 1)
    h, k, l = h * sign, k * sign, l * sign
    if not split:
        l = jnp.where(lax.axis_index("row") == 0, l, 0)
    n = jnp.where(k < HMAX, (h + HMAX) * SIDE + k + HMAX, FOLD + HMAX + h)
    l_col, is_re = l_column()
    of_l = jnp.where(l.astype(F32) == l_col, 1.0, 0.0).astype(BF16)
    of_pair = jnp.where(n == iota((PAIRS, n.shape[1]), 0), 1.0, 0.0).astype(BF16)
    times = mm(of_l, of_pair, NT)
    hf, kf = pair_rows()
    two_pi = 2.0 * math.pi
    px, py, pz = two_pi * hf, two_pi * kf, two_pi * l_col / BOX_Z
    k2 = px * px + py * py + pz * pz
    weight = jnp.exp(-k2 / (4.0 * EWALD_BETA * EWALD_BETA)) / k2
    tiles_out(mult, times * weight, tile_count)
    fill_pairs(coords[0:1], coords[1:2], tables)
    cz, sz = turns(l_col, coords[2:3])
    v1h, v1l = split2(q * jnp.where(is_re, cz, sz))
    v2h, v2l = split2(q * jnp.where(is_re, -sz, cz))
    uch, ucl, ush, usl = (t[...] for t in tables)
    total = mm(v1l, uch, NT) + mm(v1h, ucl, NT) + mm(v2l, ush, NT) + mm(v2h, usl, NT)
    total = total + (mm(v1h, uch, NT) + mm(v2h, ush, NT))
    tiles_out(sums, total, tile_count)


def exchange_kernel(
    devices, rows, cap,
    sums, mult, posts,
    grid, atoms,
    got_m, got_p, got_t, own, m_s, m_r, p_s, p_r, t_s, t_r, g_s, g_r,
):
    me = lax.axis_index("blk") * rows + lax.axis_index("row")
    share = sums.shape[0] // devices
    per_tile = 128 // cap

    def to(o):
        d = (me + o) % devices
        return d, {"blk": d // rows, "row": d % rows}

    barrier = pltpu.get_barrier_semaphore()

    @pl.loop(1, devices)
    def _(o):
        pl.semaphore_signal(
            barrier, inc=1, device_id=to(o)[1], device_id_type=pl.DeviceIdType.MESH
        )

    pl.semaphore_wait(barrier, devices - 1)

    def copy(src, dst, s, r, o, dev):
        return pltpu.make_async_remote_copy(
            src_ref=src, dst_ref=dst, send_sem=s.at[o], recv_sem=r.at[o],
            device_id=dev, device_id_type=pl.DeviceIdType.MESH,
        )

    def mult_copy(o):
        d, dev = to(o)
        return copy(mult.at[pl.ds(d * share, share)], got_m.at[o], m_s, m_r, o, dev)

    def post_copy(o):
        d, dev = to(o)
        return copy(posts.at[d], got_p.at[o], p_s, p_r, o, dev)

    def sums_copy(o):
        d, dev = to(o)
        return copy(sums.at[pl.ds(d * share, share)], got_t.at[o], t_s, t_r, o, dev)

    def grid_copy(o):
        _, dev = to(o)
        return copy(own, grid.at[pl.ds(me * share, share)], g_s, g_r, o, dev)

    def each(f):
        @pl.loop(1, devices)
        def _(o):
            f(o)

    each(lambda o: sums_copy(o).start())
    each(lambda o: mult_copy(o).start())
    each(lambda o: post_copy(o).start())
    got_t[0] = sums[pl.ds(me * share, share)]
    got_m[0] = mult[pl.ds(me * share, share)]
    got_p[0] = posts[me]
    each(lambda o: sums_copy(o).wait_recv())
    each(lambda o: mult_copy(o).wait_recv())
    piece = jnp.sum(got_t[...], axis=0) * jnp.sum(got_m[...], axis=0)
    own[...] = piece
    each(lambda o: grid_copy(o).start())
    grid[pl.ds(me * share, share)] = piece
    each(lambda o: post_copy(o).wait_recv())
    for t in range(atoms.shape[0]):
        tile = jnp.zeros((8, 128), F32)
        for s in range(t * per_tile, min((t + 1) * per_tile, devices)):
            tile = tile + got_p[(me - s + devices) % devices]
        atoms[t] = tile
    each(lambda o: grid_copy(o).wait_recv())
    each(lambda o: sums_copy(o).wait_send())
    each(lambda o: mult_copy(o).wait_send())
    each(lambda o: post_copy(o).wait_send())
    each(lambda o: grid_copy(o).wait_send())


def force_kernel(
    scale,
    coords, charges, counts, recv_index, grid, arrived,
    slot_forces, atom_forces,
    *tables,
):
    slots = coords.shape[1]
    atoms = recv_index.shape[1]
    live = iota((1, slots), 1) < counts[...]
    q = jnp.where(live, charges[...], 0.0)
    table = jnp.concatenate([arrived[t] for t in range(arrived.shape[0])], axis=1)
    index = recv_index[...]
    picks = jnp.where(index == iota((table.shape[1], atoms), 0), 1.0, 0.0).astype(BF16)
    rows = sum(mm(term, picks, NN) for term in split3(table))
    frac = [jnp.concatenate([coords[i : i + 1], rows[i : i + 1]], axis=1) for i in range(3)]
    charge = jnp.concatenate([q, rows[3:4]], axis=1)
    fill_pairs(frac[0], frac[1], tables)
    l_col, is_re = l_column()
    cz, sz = turns(l_col, frac[2])
    vf = jnp.where(is_re, sz, cz)
    hf, kf = pair_rows()
    tile = lambda i, j: grid[i * P_TILES + j]
    g = jnp.concatenate(
        [jnp.concatenate([tile(i, j) for j in range(P_TILES)], axis=1) for i in range(L_TILES)]
    )
    swap = jnp.concatenate(
        [
            part
            for i in range(L_TILES)
            for part in (g[8 * i + 4 : 8 * i + 8], g[8 * i : 8 * i + 4])
        ]
    )
    gc = jnp.where(is_re, g, -g)
    gch, gcl = split2(jnp.concatenate([gc, gc * hf, gc * kf]))
    gsh, gsl = split2(jnp.concatenate([swap, swap * hf, swap * kf]))
    uch, ucl, ush, usl = (t[...] for t in tables)
    x = mm(gcl, uch, NN) + mm(gch, ucl, NN) + mm(gsl, ush, NN) + mm(gsh, usl, NN)
    x = x + (mm(gch, uch, NN) + mm(gsh, ush, NN))
    x = x * jnp.concatenate([vf] * 3)
    two_pi = 2.0 * math.pi
    fz = jnp.sum(x[:L_ROWS] * (two_pi * l_col / BOX_Z), axis=0, keepdims=True)
    fx = two_pi * jnp.sum(x[L_ROWS : 2 * L_ROWS], axis=0, keepdims=True)
    fy = two_pi * jnp.sum(x[2 * L_ROWS :], axis=0, keepdims=True)
    force = scale * charge * jnp.concatenate([fx, fy, fz])
    slot_forces[...] = jnp.where(live, force[:, :slots], 0.0)
    atom_forces[...] = force[:, slots:]


VMEM = pl.BlockSpec(memory_space=pltpu.VMEM)


def body(coords, charges, counts, send_slot, recv_index, wave_ints):
    slots = charges.shape[0]
    atoms_dev = recv_index.shape[0]
    blks, rows = lax.axis_size("blk"), lax.axis_size("row")
    devices = blks * rows
    cap = 2 * atoms_dev // devices
    share = -(-TILES // devices)
    tile_count = share * devices
    arrivals = devices * cap // 128
    scale = FORCE_GAIN / math.sqrt(float(atoms_dev * devices * blks * wave_ints.shape[1]))
    q, count = charges[None, :], counts[:, None]
    shape = jax.ShapeDtypeStruct
    big = pltpu.CompilerParams(vmem_limit_bytes=56 * 2**20)
    sums, mult, posts = pl.pallas_call(
        functools.partial(local_kernel, devices, rows, cap, tile_count),
        out_shape=[
            shape((tile_count, 8, 128), F32),
            shape((tile_count, 8, 128), F32),
            shape((devices, 8, 128), F32),
        ],
        in_specs=[VMEM] * 5,
        out_specs=[VMEM] * 3,
        scratch_shapes=[pltpu.VMEM((PAIRS, slots), BF16)] * 4,
        compiler_params=big,
    )(coords, q, count, send_slot[None, :], wave_ints)
    dma = pltpu.SemaphoreType.DMA((devices,))
    grid, arrived = pl.pallas_call(
        functools.partial(exchange_kernel, devices, rows, cap),
        out_shape=[shape((tile_count, 8, 128), F32), shape((arrivals, 8, 128), F32)],
        in_specs=[VMEM] * 3,
        out_specs=[VMEM] * 2,
        scratch_shapes=[
            pltpu.VMEM((devices, share, 8, 128), F32),
            pltpu.VMEM((devices, 8, 128), F32),
            pltpu.VMEM((devices, share, 8, 128), F32),
            pltpu.VMEM((share, 8, 128), F32),
        ]
        + [dma] * 8,
        compiler_params=pltpu.CompilerParams(
            collective_id=0, has_side_effects=True, vmem_limit_bytes=56 * 2**20
        ),
    )(sums, mult, posts)
    return pl.pallas_call(
        functools.partial(force_kernel, scale),
        out_shape=[shape((3, slots), F32), shape((3, atoms_dev), F32)],
        in_specs=[VMEM] * 6,
        out_specs=[VMEM] * 2,
        scratch_shapes=[pltpu.VMEM((PAIRS, slots + atoms_dev), BF16)] * 4,
        compiler_params=big,
    )(coords, q, count, recv_index[None, :], grid, arrived)


def solution(mesh):
    ions = P(("groups", "blk", "row"))
    return jax.shard_map(
        body,
        mesh=mesh,
        in_specs=(P(None, *ions), ions, ions, ions, ions, P(None, "blk")),
        out_specs=(P(None, *ions), P(None, *ions)),
        check_vma=False,
    )
```

time: 504 us -> 40.4 us (0.08)
  other arithmetic: 431 us -> 0 us
  Pallas kernels: 0 us -> 37.1 us
  blocking collectives: 34.6 us -> 0 us
  local copies, waits for them, and re-layouts: 15.5 us -> 1.26 us
  starting transfers between devices: 11 us -> 0 us
  waiting for transfers between devices: 9.79 us -> 0 us
    reduce_sum x3 -> x0, other arithmetic: 231 us -> none  [the longest x1 214 us: phase_sums(): jnp.sum(atom_rows[3][None, :] * jnp.cos(angles), axis=1)]
    sub x1 -> x0, other arithmetic: 193 us -> none  [pull_sum(): jnp.sin(angles) * cos_weighted[:, None]]
    pallas_call x0 -> x3, Pallas kernels: none -> 37.1 us  [the longest x1 25.9 us: body(): pl.pallas_call(functools.partial(exchange_kernel, devices, rows, cap), ou...]
    all_gather x2 -> x0, blocking collectives: 21.6 us -> none  [the longest x1 11.4 us: body(): shard_piece = lax.all_gather(package, 'blk', axis=1, tiled=True)]
    psum x1 -> x0, blocking collectives: 13 us -> none  [body(): cos_sum, sin_sum = lax.psum((cos_part, sin_part), 'row')]
    all_to_all x2 -> x0, starting transfers between devices: 11 us -> none  [the longest x1 7.35 us: body(): lax.all_to_all(outgoing.reshape(4, devices, pair_cap), ('blk', 'row'), sp...]
    all_to_all x2 -> x0, waiting for transfers between devices: 9.79 us -> none  [the longest x1 5.53 us: body(): lax.all_to_all(homeward.reshape(3, devices, pair_cap), ('blk', 'row'), sp...]
    scatter x2 -> x0, local copies, waits for them, and re-layouts: 6.13 us -> none  [the longest x1 4.29 us: body(): jnp.zeros((4, buf_width), jnp.float32).at[:, target_slot]]
  transfers between devices with their start and end apart: 2 -> 0, of which waited for: 2 -> 0; matrix products, arithmetic and copies ran while one was open for 0% -> 0% of each run, Pallas kernels for 0% -> 0%
where the time goes in v1:
time: 40.4 us; the launch traced here: 39.7 us
  Pallas kernels  37.1 us (92%)
  between operations  1.32 us (3%)
  local copies, waits for them, and re-layouts  1.26 us (3%)
    pallas_call x1, Pallas kernels, body(): pl.pallas_call(functools.partial(exchange_kernel, devices, rows, cap), ou...  25.9 us
    pallas_call x1, Pallas kernels, body(): pl.pallas_call(functools.partial(local_kernel, devices, rows, cap, tile_c...  5.72 us
    pallas_call x1, Pallas kernels, body(): pl.pallas_call(functools.partial(force_kernel, scale), out_shape=[shape((...  5.52 us

profile of v1, /device:TPU:1, one launch (start us, length us, event | category | flops | bytes accessed | tf_op | source)
XLA Modules:
  0.0 39.7 jit_solution(7578086702261206376)
XLA Ops:
  0.6 0.0 copy-start
  1.3 0.0 copy-start.1
  1.3 0.0 copy-done
  1.3 0.6 %broadcast_in_dim.12.charges = f32[1,768]{1,0:T(1,128)} reshape(f32[768]{0:T(1024)S(1)} %copy-done) | data formatting | bytes 6144 | tf_op jit(solution)/shard_map/broadcast_in_dim | solution.py:315
  1.9 0.1 copy-done.1
  2.0 0.6 %broadcast_in_dim.15.send_slot = s32[1,768]{1,0:T(1,128)} reshape(s32[768]{0:T(1024)S(1)} %copy-done.1) | data formatting | bytes 6144 | tf_op jit(solution)/shard_map/broadcast_in_dim | solution.py:329
  2.6 5.7 %shard_map.77 = (f32[48,8,128]{2,1,0:T(8,128)}, f32[48,8,128]{2,1,0:T(8,128)}, f32[16,8,128]{2,1,0:T(8,128)}) custom-call(f32[3,768]{1,0:T(4,128)} %coords.3, f32[1,768]{1,0:T(1,128)} %broadcast_in_dim.12.charges, s32[1,1]{1,0:T(1,128)} %bitcast.2.counts, s32[1,768]{1,0:T(1,128)} %broadcast_in_dim.15.send_slot, s32[3,6144]{1,0:T(4,128)} %wave.1), custom_call_target="tpu_custom_call" | custom-call | tf_op jit(solution)/shard_map/pallas_call | solution.py:318
  8.3 25.9 %shard_map.78 = (f32[48,8,128]{2,1,0:T(8,128)}, f32[8,8,128]{2,1,0:T(8,128)}) custom-call(f32[48,8,128]{2,1,0:T(8,128)} %get-tuple-element.7.sums, f32[48,8,128]{2,1,0:T(8,128)} %get-tuple-element.8.mult, f32[16,8,128]{2,1,0:T(8,128)} %get-tuple-element.9.posts), custom_call_target="tpu_custom_call" | custom-call | tf_op jit(solution)/shard_map/pallas_call | solution.py:331
  34.2 5.5 %shard_map.79 = (f32[3,768]{1,0:T(4,128)}, f32[3,512]{1,0:T(4,128)}) custom-call(f32[3,768]{1,0:T(4,128)} %coords.3, f32[1,768]{1,0:T(1,128)} %broadcast_in_dim.12.charges, s32[1,1]{1,0:T(1,128)} %bitcast.3.counts, s32[1,512]{1,0:T(1,128)} %bitcast.4, f32[48,8,128]{2,1,0:T(8,128)} %get-tuple-element.10.grid, f32[8,8,128]{2,1,0:T(8,128)} %get-tuple-element.11.arrived), custom_call_target="tpu_custom_call" | custom-call | tf_op jit(solution)/shard_map/pallas_call | solution.py:347
Async XLA Ops:
  0.6 0.7 %copy-start = (f32[768]{0:T(1024)S(1)}, f32[768]{0:T(1024)}, u32[]{:S(2)}) copy-start(f32[768]{0:T(1024)} %param.7) | copy-start | bytes 9220
  1.3 0.7 %copy-start.1 = (s32[768]{0:T(1024)S(1)}, s32[768]{0:T(1024)}, u32[]{:S(2)}) copy-start(s32[768]{0:T(1024)} %param.9) | copy-start | bytes 9220

commit v2 on v1

v2 whole, which is shorter than its diff:
```python
import functools
import math

import jax
import jax.numpy as jnp
from jax import lax
from jax.experimental import pallas as pl
from jax.experimental.pallas import tpu as pltpu
from jax.sharding import PartitionSpec as P

EWALD_BETA = 30.0
BOX_Z = 3.0
FORCE_GAIN = 400.0
HMAX = 12
LMAX = 36
SIDE = 2 * HMAX
FOLD = (2 * HMAX + 1) * SIDE
PAIRS = 640
L_ROWS = 2 * LMAX
L_TILES = L_ROWS // 8
P_TILES = PAIRS // 128
TILES = L_TILES * P_TILES
F32 = jnp.float32
BF16 = jnp.bfloat16

SIN_C = [(-1) ** n * math.pi ** (2 * n + 1) / math.factorial(2 * n + 1) for n in range(7)]
COS_C = [(-1) ** n * math.pi ** (2 * n) / math.factorial(2 * n) for n in range(8)]
NT = (((1,), (1,)), ((), ()))
NN = (((1,), (0,)), ((), ()))


def iota(shape, dim):
    return lax.broadcasted_iota(jnp.int32, shape, dim)


def horner(coefs, u):
    out = jnp.full_like(u, coefs[-1])
    for c in coefs[-2::-1]:
        out = out * u + c
    return out


def turns(mult, frac):
    high = jnp.floor(frac * 4096.0 + 0.5) * (1.0 / 4096.0)
    low = frac - high
    whole = mult * high
    r = (whole - jnp.floor(whole + 0.5)) + mult * low
    u = r * r
    s = r * horner(SIN_C, u)
    c = horner(COS_C, u)
    return 1.0 - 2.0 * s * s, 2.0 * s * c


def split2(x):
    hi = x.astype(BF16)
    return hi, (x - hi.astype(F32)).astype(BF16)


def split3(x):
    hi = x.astype(BF16)
    rest = x - hi.astype(F32)
    mid = rest.astype(BF16)
    return hi, mid, (rest - mid.astype(F32)).astype(BF16)


def mm(a, b, dims):
    return lax.dot_general(a, b, dims, preferred_element_type=F32)


def l_column():
    row = iota((L_ROWS, 1), 0)
    return (4 * (row // 8) + row % 4 + 1).astype(F32), (row % 8) < 4


def pair_rows():
    n = iota((1, PAIRS), 1)
    tall = n < FOLD
    q = n // SIDE
    h = jnp.where(tall, q - HMAX, n - FOLD - HMAX)
    k = jnp.where(tall, n - q * SIDE - HMAX, HMAX)
    return h.astype(F32), k.astype(F32)


def fill_pairs(frac_x, frac_y, tables, first):
    width = frac_x.shape[1]
    lanes = pl.ds(first, width)
    mult = (iota((32, 1), 0) - HMAX).astype(F32)
    cx, sx = turns(mult, frac_x)
    cy, sy = turns(mult, frac_y)
    cyk, syk = cy[:SIDE], sy[:SIDE]

    def put(start, c, s):
        rows = pl.ds(start, c.shape[0])
        for value, (hi_ref, lo_ref) in ((c, tables[:2]), (s, tables[2:])):
            hi, lo = split2(value)
            hi_ref[rows, lanes] = hi
            lo_ref[rows, lanes] = lo

    def one(i):
        a, b = cx[i : i + 1], sx[i : i + 1]
        return a * cyk - b * syk, b * cyk + a * syk

    for i in range(0, 2 * HMAX, 2):
        (c0, s0), (c1, s1) = one(i), one(i + 1)
        put(i * SIDE, jnp.concatenate([c0, c1]), jnp.concatenate([s0, s1]))
    c0, s0 = one(2 * HMAX)
    a, b = cy[SIDE : SIDE + 1], sy[SIDE : SIDE + 1]
    pad = jnp.zeros((8, width), F32)
    put(
        2 * HMAX * SIDE,
        jnp.concatenate([c0, cx * a - sx * b, pad]),
        jnp.concatenate([s0, sx * a + cx * b, pad]),
    )


def tiles_out(ref, value, count):
    for t in range(count):
        if t < TILES:
            i, j = t // P_TILES, t % P_TILES
            ref[t] = value[8 * i : 8 * i + 8, 128 * j : 128 * j + 128]
        else:
            ref[t] = jnp.zeros((8, 128), F32)


def each(count, f):
    if count <= 16:
        for o in range(1, count):
            f(o)
    else:
        pl.loop(1, count)(f)


def kernel(
    blks, rows, cap, scale,
    coords, charges, counts, send_slot, recv_index, wave,
    slot_forces, atom_forces,
    uch_ref, ucl_ref, ush_ref, usl_ref, mail, got_mail, sums, from_sib, half_sums, got_t, own, grid,
    m_s, m_r, x_s, x_r, t_s, t_r, g_s, g_r, f_s, f_r,
):
    devices = blks * rows
    chips = devices // 2
    slots = coords.shape[1]
    atoms = recv_index.shape[0]
    blk, row = lax.axis_index("blk"), lax.axis_index("row")
    me = blk * rows + row
    core = blk % 2
    chip = blk // 2 * rows + row
    share = own.shape[0]
    half = chips * share
    tile_count = 2 * half
    mine = core * half
    tables = (uch_ref, ucl_ref, ush_ref, usl_ref)
    mesh_id = pl.DeviceIdType.MESH
    sibling = {"blk": blk + 1 - 2 * core, "row": row}

    def other(o):
        d = (me + o) % devices
        return d, {"blk": d // rows, "row": d % rows}

    def other_chip(o):
        c = (chip + o) % chips
        return c, {"blk": c // rows * 2 + core, "row": c % rows}

    def copy(src, dst, s, r, o, dev):
        return pltpu.make_async_remote_copy(
            src_ref=src, dst_ref=dst, send_sem=s.at[o], recv_sem=r.at[o],
            device_id=dev, device_id_type=mesh_id,
        )

    def mail_copy(o):
        d, dev = other(o)
        return copy(mail.at[d], got_mail.at[o], m_s, m_r, o, dev)

    def sib_copy():
        return copy(sums.at[pl.ds(half - mine, half)], from_sib, x_s, x_r, 0, sibling)

    def sums_copy(o):
        c, dev = other_chip(o)
        return copy(half_sums.at[pl.ds(c * share, share)], got_t.at[o], t_s, t_r, o, dev)

    def grid_copy(o):
        _, dev = other_chip(o)
        return copy(own, grid.at[pl.ds(mine + chip * share, share)], g_s, g_r, o, dev)

    def pass_on(o):
        c = (chip + chips - o) % chips
        place = grid.at[pl.ds(mine + c * share, share)]
        return copy(own if isinstance(o, int) and o == 0 else place, place, f_s, f_r, o, sibling)

    barrier = pltpu.get_barrier_semaphore()
    each(
        devices,
        lambda o: pl.semaphore_signal(
            barrier, inc=1, device_id=other(o)[1], device_id_type=mesh_id
        ),
    )

    live = iota((1, slots), 1) < counts[0]
    q = jnp.where(live, charges[...].reshape(1, slots), 0.0)
    target = jnp.where(live, send_slot[...].reshape(1, slots), -1)
    spots = jnp.where(target == iota((devices * cap, slots), 0), 1.0, 0.0).astype(BF16)
    entries = jnp.concatenate([coords[...], q, jnp.zeros((4, slots), F32)])
    out = sum(mm(term, spots, NT) for term in split3(entries))
    per_tile = 128 // cap
    lane_part = iota((8, 128), 1) // cap
    for d in range(devices):
        tile = out[:, 128 * (d // per_tile) : 128 * (d // per_tile) + 128]
        tile = jnp.where(lane_part == d % per_tile, tile, 0.0)
        shift = (me % per_tile - d % per_tile + per_tile) % per_tile * cap
        mail[d, share] = pltpu.roll(tile, shift, 1)[:4]
    k_local = wave.shape[1]
    part = k_local // rows
    split = part % 128 == 0 and part * rows == k_local
    w = wave[:, pl.ds(pl.multiple_of(row * part, 128), part)] if split else wave[...]
    h, k, l = w[0:1], w[1:2], w[2:3]
    sign = jnp.where(l < 0, -1, 1)
    h, k, l = h * sign, k * sign, l * sign
    if not split:
        l = jnp.where(row == 0, l, 0)
    n = jnp.where(k < HMAX, (h + HMAX) * SIDE + k + HMAX, FOLD + HMAX + h)
    l_col, is_re = l_column()
    of_l = jnp.where(l.astype(F32) == l_col, 1.0, 0.0).astype(BF16)
    of_pair = jnp.where(n == iota((PAIRS, n.shape[1]), 0), 1.0, 0.0).astype(BF16)
    times = mm(of_l, of_pair, NT)
    hf, kf = pair_rows()
    two_pi = 2.0 * math.pi
    px, py, pz = two_pi * hf, two_pi * kf, two_pi * l_col / BOX_Z
    k2 = px * px + py * py + pz * pz
    times = times * (jnp.exp(-k2 / (4.0 * EWALD_BETA * EWALD_BETA)) / k2)
    for t in range(tile_count):
        c, piece = t // half, t % half // share
        d = (piece // rows * 2 + c) * rows + piece % rows
        if t < TILES:
            i, j = t // P_TILES, t % P_TILES
            mail[d, t % share] = times[8 * i : 8 * i + 4, 128 * j : 128 * j + 128]
        else:
            mail[d, t % share] = jnp.zeros((4, 128), F32)
    pl.semaphore_wait(barrier, devices - 1)
    each(devices, lambda o: mail_copy(o).start())

    fill_pairs(coords[0:1], coords[1:2], tables, 0)
    cz, sz = turns(l_col, coords[2:3])
    v1h, v1l = split2(q * jnp.where(is_re, cz, sz))
    v2h, v2l = split2(q * jnp.where(is_re, -sz, cz))
    uch, ucl, ush, usl = (t[:, :slots] for t in tables)
    total = mm(v1l, uch, NT) + mm(v1h, ucl, NT) + mm(v2l, ush, NT) + mm(v2h, usl, NT)
    total = total + (mm(v1h, uch, NT) + mm(v2h, ush, NT))
    for t in range(tile_count):
        if t < TILES:
            i, j = t // P_TILES, t % P_TILES
            sums[t] = total[8 * i : 8 * i + 8, 128 * j : 128 * j + 128]
        else:
            sums[t] = jnp.zeros((8, 128), F32)
    sib_copy().start()

    each(devices, lambda o: mail_copy(o).wait_recv())
    got_mail[0] = mail[me]
    arrived = []
    for t in range(devices // per_tile):
        tile = jnp.zeros((4, 128), F32)
        for s in range(t * per_tile, (t + 1) * per_tile):
            tile = tile + got_mail[(me - s + devices) % devices, share]
        arrived.append(tile)
    table = jnp.concatenate(arrived, axis=1)
    table = jnp.concatenate([table, jnp.zeros_like(table)])
    index = recv_index[...].reshape(1, atoms)
    picks = jnp.where(index == iota((table.shape[1], atoms), 0), 1.0, 0.0).astype(BF16)
    ions = sum(mm(term, picks, NN) for term in split3(table))
    m_own = got_mail[0, :share]
    for o in range(1, devices):
        m_own = m_own + got_mail[o, :share]

    sib_copy().wait_recv()
    half_sums[...] = sums[pl.ds(mine, half)] + from_sib[...]
    each(chips, lambda o: sums_copy(o).start())
    fill_pairs(ions[0:1], ions[1:2], tables, slots)
    each(chips, lambda o: sums_copy(o).wait_recv())
    got_t[0] = half_sums[pl.ds(chip * share, share)]
    piece = jnp.sum(got_t[...], axis=0) * jnp.concatenate([m_own, m_own], axis=1)
    own[...] = piece
    each(chips, lambda o: grid_copy(o).start())
    pass_on(0).start()
    grid[pl.ds(mine + chip * share, share)] = piece
    cz2, sz2 = turns(l_col, ions[2:3])
    vf = jnp.where(is_re, jnp.concatenate([sz, sz2], axis=1), jnp.concatenate([cz, cz2], axis=1))
    charge = jnp.concatenate([q, ions[3:4]], axis=1)

    def forward(o):
        grid_copy(o).wait_recv()
        pass_on(o).start()

    each(chips, forward)
    pass_on(0).wait_recv()
    each(chips, lambda o: pass_on(o).wait_recv())

    tile = lambda i, j: grid[i * P_TILES + j]
    g = jnp.concatenate(
        [jnp.concatenate([tile(i, j) for j in range(P_TILES)], axis=1) for i in range(L_TILES)]
    )
    swap = jnp.concatenate(
        [
            rows4
            for i in range(L_TILES)
            for rows4 in (g[8 * i + 4 : 8 * i + 8], g[8 * i : 8 * i + 4])
        ]
    )
    gc = jnp.where(is_re, g, -g)
    gch, gcl = split2(jnp.concatenate([gc, gc * hf, gc * kf]))
    gsh, gsl = split2(jnp.concatenate([swap, swap * hf, swap * kf]))
    uch, ucl, ush, usl = (t[...] for t in tables)
    x = mm(gcl, uch, NN) + mm(gch, ucl, NN) + mm(gsl, ush, NN) + mm(gsh, usl, NN)
    x = x + (mm(gch, uch, NN) + mm(gsh, ush, NN))
    x = x * jnp.concatenate([vf] * 3)
    fz = jnp.sum(x[:L_ROWS] * (two_pi * l_col / BOX_Z), axis=0, keepdims=True)
    fx = two_pi * jnp.sum(x[L_ROWS : 2 * L_ROWS], axis=0, keepdims=True)
    fy = two_pi * jnp.sum(x[2 * L_ROWS :], axis=0, keepdims=True)
    force = scale * charge * jnp.concatenate([fx, fy, fz])
    slot_forces[...] = jnp.where(live, force[:, :slots], 0.0)
    atom_forces[...] = force[:, slots:]

    each(devices, lambda o: mail_copy(o).wait_send())
    sib_copy().wait_send()
    each(chips, lambda o: sums_copy(o).wait_send())
    each(chips, lambda o: grid_copy(o).wait_send())
    pass_on(0).wait_send()
    each(chips, lambda o: pass_on(o).wait_send())


VMEM = pl.BlockSpec(memory_space=pltpu.VMEM)
SMEM = pl.BlockSpec(memory_space=pltpu.SMEM)


def body(coords, charges, counts, send_slot, recv_index, wave_ints):
    slots = charges.shape[0]
    atoms = recv_index.shape[0]
    blks, rows = lax.axis_size("blk"), lax.axis_size("row")
    devices = blks * rows
    chips = devices // 2
    cap = 2 * atoms // devices
    share = -(-TILES // devices)
    half = chips * share
    scale = FORCE_GAIN / math.sqrt(float(atoms * devices * blks * wave_ints.shape[1]))
    shape = jax.ShapeDtypeStruct
    dma = lambda n: [pltpu.SemaphoreType.DMA((n,))] * 2
    return pl.pallas_call(
        functools.partial(kernel, blks, rows, cap, scale),
        out_shape=[shape((3, slots), F32), shape((3, atoms), F32)],
        in_specs=[VMEM, VMEM, SMEM, VMEM, VMEM, VMEM],
        out_specs=[VMEM] * 2,
        scratch_shapes=[pltpu.VMEM((PAIRS, slots + atoms), BF16)] * 4
        + [
            pltpu.VMEM((devices, share + 1, 4, 128), F32),
            pltpu.VMEM((devices, share + 1, 4, 128), F32),
            pltpu.VMEM((2 * half, 8, 128), F32),
            pltpu.VMEM((half, 8, 128), F32),
            pltpu.VMEM((half, 8, 128), F32),
            pltpu.VMEM((chips, share, 8, 128), F32),
            pltpu.VMEM((share, 8, 128), F32),
            pltpu.VMEM((2 * half, 8, 128), F32),
        ]
        + dma(devices) + dma(1) + dma(chips) + dma(chips) + dma(chips),
        compiler_params=pltpu.CompilerParams(
            collective_id=0, has_side_effects=True, vmem_limit_bytes=56 * 2**20
        ),
    )(coords, charges, counts, send_slot, recv_index, wave_ints)


def solution(mesh):
    ions = P(("groups", "blk", "row"))
    return jax.shard_map(
        body,
        mesh=mesh,
        in_specs=(P(None, *ions), ions, ions, ions, ions, P(None, "blk")),
        out_specs=(P(None, *ions), P(None, *ions)),
        check_vma=False,
    )
```

time: 40.4 us -> 32.4 us (0.80); the launches traced: 39.7 us -> 32.2 us
  Pallas kernels: 37.1 us -> 29 us
  local copies, waits for them, and re-layouts: 1.26 us -> 1.92 us
    pallas_call x3 -> x1, Pallas kernels: 37.1 us -> 29 us  [body(): pl.pallas_call(functools.partial(kernel, blks, rows, cap, scale), out_sha...]
    unnamed x4, local copies, waits for them, and re-layouts: 0.1 us -> 1.92 us
    broadcast_in_dim x2 -> x0, local copies, waits for them, and re-layouts: 1.16 us -> none  [the longest x1 0.58 us: body(): send_slot[None, :]]
where the time goes in v2:
time: 32.4 us; the launch traced here: 32.2 us
  Pallas kernels  29 us (90%)
  local copies, waits for them, and re-layouts  1.92 us (6%)
  between operations  1.29 us (4%)
    pallas_call x1, Pallas kernels, body(): pl.pallas_call(functools.partial(kernel, blks, rows, cap, scale), out_sha...  29 us
    unnamed x4, local copies, waits for them, and re-layouts  1.92 us

profile of v2, /device:TPU:1, one launch (start us, length us, event | category | flops | bytes accessed | tf_op | source)
XLA Modules:
  0.0 32.2 jit_solution(13600817502469123520)
XLA Ops:
  1.3 29.0 %shard_map.77 = (f32[3,768]{1,0:T(4,128)}, f32[3,512]{1,0:T(4,128)}) custom-call(f32[3,768]{1,0:T(4,128)} %coords.1, f32[768]{0:T(1024)} %charges.1, s32[1]{0:T(128)S(6)} %copy.10.counts, s32[768]{0:T(1024)} %send_slot.1, s32[512]{0:T(512)} %recv_index.1, s32[3,6144]{1,0:T(4,128)} %wave.1), custom_call_target="tpu_custom_call" | custom-call | tf_op jit(solution)/shard_map/pallas_call | solution.py:345
  30.3 0.0 copy-start
  30.3 1.3 %copy.11 = f32[3,768]{1,0:T(4,128)} copy(f32[3,768]{1,0:T(4,128)} %get-tuple-element.4) | data formatting | bytes 18432
  31.6 0.0 copy-done
  31.6 0.6 %copy.12 = f32[3,512]{1,0:T(4,128)} copy(f32[3,512]{1,0:T(4,128)S(1)} %copy-done) | data formatting | bytes 12288
Async XLA Ops:
  30.3 1.3 %copy-start = (f32[3,512]{1,0:T(4,128)S(1)}, f32[3,512]{1,0:T(4,128)}, u32[]{:S(2)}) copy-start(f32[3,512]{1,0:T(4,128)} %get-tuple-element.5) | copy-start | bytes 18436

commit v3 on v2

--- a/solution.py
+++ b/solution.py
@@ -81,7 +81,7 @@
     return h.astype(F32), k.astype(F32)
 
 
-def fill_pairs(frac_x, frac_y, tables, first):
+def fill_pairs(frac_x, frac_y, table, first):
     width = frac_x.shape[1]
     lanes = pl.ds(first, width)
     mult = (iota((32, 1), 0) - HMAX).astype(F32)
@@ -90,11 +90,10 @@
     cyk, syk = cy[:SIDE], sy[:SIDE]
 
     def put(start, c, s):
-        rows = pl.ds(start, c.shape[0])
-        for value, (hi_ref, lo_ref) in ((c, tables[:2]), (s, tables[2:])):
+        for part, value in enumerate((c, s)):
             hi, lo = split2(value)
-            hi_ref[rows, lanes] = hi
-            lo_ref[rows, lanes] = lo
+            table[pl.ds(part * PAIRS + start, c.shape[0]), lanes] = hi
+            table[pl.ds((part + 2) * PAIRS + start, c.shape[0]), lanes] = lo
 
     def one(i):
         a, b = cx[i : i + 1], sx[i : i + 1]
@@ -133,8 +132,8 @@
 def kernel(
     blks, rows, cap, scale,
     coords, charges, counts, send_slot, recv_index, wave,
-    slot_forces, atom_forces,
-    uch_ref, ucl_ref, ush_ref, usl_ref, mail, got_mail, sums, from_sib, half_sums, got_t, own, grid,
+    forces,
+    table, mail, got_mail, sums, from_sib, half_sums, got_t, own, grid,
     m_s, m_r, x_s, x_r, t_s, t_r, g_s, g_r, f_s, f_r,
 ):
     devices = blks * rows
@@ -149,7 +148,6 @@
     half = chips * share
     tile_count = 2 * half
     mine = core * half
-    tables = (uch_ref, ucl_ref, ush_ref, usl_ref)
     mesh_id = pl.DeviceIdType.MESH
     sibling = {"blk": blk + 1 - 2 * core, "row": row}
 
@@ -235,14 +233,14 @@
             mail[d, t % share] = times[8 * i : 8 * i + 4, 128 * j : 128 * j + 128]
         else:
             mail[d, t % share] = jnp.zeros((4, 128), F32)
+
+    fill_pairs(coords[0:1], coords[1:2], table, 0)
     pl.semaphore_wait(barrier, devices - 1)
     each(devices, lambda o: mail_copy(o).start())
-
-    fill_pairs(coords[0:1], coords[1:2], tables, 0)
     cz, sz = turns(l_col, coords[2:3])
     v1h, v1l = split2(q * jnp.where(is_re, cz, sz))
     v2h, v2l = split2(q * jnp.where(is_re, -sz, cz))
-    uch, ucl, ush, usl = (t[:, :slots] for t in tables)
+    uch, ush, ucl, usl = (table[pl.ds(i * PAIRS, PAIRS), :slots] for i in range(4))
     total = mm(v1l, uch, NT) + mm(v1h, ucl, NT) + mm(v2l, ush, NT) + mm(v2h, usl, NT)
     total = total + (mm(v1h, uch, NT) + mm(v2h, ush, NT))
     for t in range(tile_count):
@@ -252,6 +250,9 @@
         else:
             sums[t] = jnp.zeros((8, 128), F32)
     sib_copy().start()
+    sib_copy().wait_recv()
+    half_sums[...] = sums[pl.ds(mine, half)] + from_sib[...]
+    each(chips, lambda o: sums_copy(o).start())
 
     each(devices, lambda o: mail_copy(o).wait_recv())
     got_mail[0] = mail[me]
@@ -261,19 +262,16 @@
         for s in range(t * per_tile, (t + 1) * per_tile):
             tile = tile + got_mail[(me - s + devices) % devices, share]
         arrived.append(tile)
-    table = jnp.concatenate(arrived, axis=1)
-    table = jnp.concatenate([table, jnp.zeros_like(table)])
+    came = jnp.concatenate(arrived, axis=1)
+    came = jnp.concatenate([came, jnp.zeros_like(came)])
     index = recv_index[...].reshape(1, atoms)
-    picks = jnp.where(index == iota((table.shape[1], atoms), 0), 1.0, 0.0).astype(BF16)
-    ions = sum(mm(term, picks, NN) for term in split3(table))
+    picks = jnp.where(index == iota((came.shape[1], atoms), 0), 1.0, 0.0).astype(BF16)
+    ions = sum(mm(term, picks, NN) for term in split3(came))
     m_own = got_mail[0, :share]
     for o in range(1, devices):
         m_own = m_own + got_mail[o, :share]
 
-    sib_copy().wait_recv()
-    half_sums[...] = sums[pl.ds(mine, half)] + from_sib[...]
-    each(chips, lambda o: sums_copy(o).start())
-    fill_pairs(ions[0:1], ions[1:2], tables, slots)
+    fill_pairs(ions[0:1], ions[1:2], table, slots)
     each(chips, lambda o: sums_copy(o).wait_recv())
     got_t[0] = half_sums[pl.ds(chip * share, share)]
     piece = jnp.sum(got_t[...], axis=0) * jnp.concatenate([m_own, m_own], axis=1)
@@ -307,16 +305,13 @@
     gc = jnp.where(is_re, g, -g)
     gch, gcl = split2(jnp.concatenate([gc, gc * hf, gc * kf]))
     gsh, gsl = split2(jnp.concatenate([swap, swap * hf, swap * kf]))
-    uch, ucl, ush, usl = (t[...] for t in tables)
-    x = mm(gcl, uch, NN) + mm(gch, ucl, NN) + mm(gsl, ush, NN) + mm(gsh, usl, NN)
-    x = x + (mm(gch, uch, NN) + mm(gsh, ush, NN))
+    x = mm(jnp.concatenate([gch, gsh] * 2, axis=1), table[...], NN)
+    x = x + mm(jnp.concatenate([gcl, gsl], axis=1), table[: 2 * PAIRS], NN)
     x = x * jnp.concatenate([vf] * 3)
     fz = jnp.sum(x[:L_ROWS] * (two_pi * l_col / BOX_Z), axis=0, keepdims=True)
     fx = two_pi * jnp.sum(x[L_ROWS : 2 * L_ROWS], axis=0, keepdims=True)
     fy = two_pi * jnp.sum(x[2 * L_ROWS :], axis=0, keepdims=True)
-    force = scale * charge * jnp.concatenate([fx, fy, fz])
-    slot_forces[...] = jnp.where(live, force[:, :slots], 0.0)
-    atom_forces[...] = force[:, slots:]
+    forces[...] = scale * charge * jnp.concatenate([fx, fy, fz])
 
     each(devices, lambda o: mail_copy(o).wait_send())
     sib_copy().wait_send()
@@ -324,6 +319,13 @@
     each(chips, lambda o: grid_copy(o).wait_send())
     pass_on(0).wait_send()
     each(chips, lambda o: pass_on(o).wait_send())
+
+
+def deliver(counts, forces, slot_forces, atom_forces):
+    slots = slot_forces.shape[1]
+    live = iota((1, slots), 1) < counts[0]
+    slot_forces[...] = jnp.where(live, forces[:, :slots], 0.0)
+    atom_forces[...] = forces[:, slots:]
 
 
 VMEM = pl.BlockSpec(memory_space=pltpu.VMEM)
@@ -342,12 +344,12 @@
     scale = FORCE_GAIN / math.sqrt(float(atoms * devices * blks * wave_ints.shape[1]))
     shape = jax.ShapeDtypeStruct
     dma = lambda n: [pltpu.SemaphoreType.DMA((n,))] * 2
-    return pl.pallas_call(
+    forces = pl.pallas_call(
         functools.partial(kernel, blks, rows, cap, scale),
-        out_shape=[shape((3, slots), F32), shape((3, atoms), F32)],
+        out_shape=shape((3, slots + atoms), F32),
         in_specs=[VMEM, VMEM, SMEM, VMEM, VMEM, VMEM],
-        out_specs=[VMEM] * 2,
-        scratch_shapes=[pltpu.VMEM((PAIRS, slots + atoms), BF16)] * 4
+        out_specs=VMEM,
+        scratch_shapes=[pltpu.VMEM((4 * PAIRS, slots + atoms), BF16)]
         + [
             pltpu.VMEM((devices, share + 1, 4, 128), F32),
             pltpu.VMEM((devices, share + 1, 4, 128), F32),
@@ -363,6 +365,12 @@
             collective_id=0, has_side_effects=True, vmem_limit_bytes=56 * 2**20
         ),
     )(coords, charges, counts, send_slot, recv_index, wave_ints)
+    return pl.pallas_call(
+        deliver,
+        out_shape=[shape((3, slots), F32), shape((3, atoms), F32)],
+        in_specs=[SMEM, VMEM],
+        out_specs=[VMEM] * 2,
+    )(counts, forces)
 
 
 def solution(mesh):

time: 32.4 us -> 27.4 us (0.85)
  Pallas kernels: 29 us -> 25.9 us
  local copies, waits for them, and re-layouts: 1.92 us -> 0 us
    pallas_call x1, Pallas kernels: 29 us -> 24.5 us  [body(): pl.pallas_call(functools.partial(kernel, blks, rows, cap, scale), out_sha...]
    unnamed x4 -> x0, local copies, waits for them, and re-layouts: 1.92 us -> none
    pallas_call x0 -> x1, Pallas kernels: none -> 1.34 us  [body(): pl.pallas_call(deliver, out_shape=[shape((3, slots), F32), shape((3, atom...]
where the time goes in v3:
time: 27.4 us; the launch traced here: 27.2 us
  Pallas kernels  25.9 us (95%)
  between operations  1.28 us (5%)
    pallas_call x1, Pallas kernels, body(): pl.pallas_call(functools.partial(kernel, blks, rows, cap, scale), out_sha...  24.5 us
    pallas_call x1, Pallas kernels, body(): pl.pallas_call(deliver, out_shape=[shape((3, slots), F32), shape((3, atom...  1.34 us

profile of v3, /device:TPU:1, one launch (start us, length us, event | category | flops | bytes accessed | tf_op | source)
XLA Modules:
  0.0 27.2 jit_solution(17652856698786664760)
XLA Ops:
  1.3 24.5 %shard_map.77.forces = f32[3,1280]{1,0:T(4,128)} custom-call(f32[3,768]{1,0:T(4,128)} %coords.1, f32[768]{0:T(1024)} %charges.1, s32[1]{0:T(128)S(6)} %copy.8.counts, s32[768]{0:T(1024)} %send_slot.1, s32[512]{0:T(512)} %recv_index.1, s32[3,6144]{1,0:T(4,128)} %wave.1), custom_call_target="tpu_custom_call" | custom-call | tf_op jit(solution)/shard_map/pallas_call | solution.py:347
  25.8 1.3 %shard_map.78 = (f32[3,768]{1,0:T(4,128)}, f32[3,512]{1,0:T(4,128)}) custom-call(s32[1]{0:T(128)S(6)} %copy.8.counts, f32[3,1280]{1,0:T(4,128)} %shard_map.77.forces), custom_call_target="tpu_custom_call" | custom-call | tf_op jit(solution)/shard_map/pallas_call | solution.py:368

commit v4 on v3

--- a/solution.py
+++ b/solution.py
@@ -198,7 +198,9 @@
     target = jnp.where(live, send_slot[...].reshape(1, slots), -1)
     spots = jnp.where(target == iota((devices * cap, slots), 0), 1.0, 0.0).astype(BF16)
     entries = jnp.concatenate([coords[...], q, jnp.zeros((4, slots), F32)])
-    out = sum(mm(term, spots, NT) for term in split3(entries))
+    terms = [*split3(entries), jnp.zeros((128 - 24, slots), BF16)]
+    out = mm(spots, jnp.concatenate(terms), NT).T
+    out = out[:8] + out[8:16] + out[16:24]
     per_tile = 128 // cap
     lane_part = iota((8, 128), 1) // cap
     for d in range(devices):
@@ -219,7 +221,8 @@
     l_col, is_re = l_column()
     of_l = jnp.where(l.astype(F32) == l_col, 1.0, 0.0).astype(BF16)
     of_pair = jnp.where(n == iota((PAIRS, n.shape[1]), 0), 1.0, 0.0).astype(BF16)
-    times = mm(of_l, of_pair, NT)
+    of_l = jnp.concatenate([of_l, jnp.zeros((128 - L_ROWS, of_l.shape[1]), BF16)])
+    times = mm(of_pair, of_l, NT).T[:L_ROWS]
     hf, kf = pair_rows()
     two_pi = 2.0 * math.pi
     px, py, pz = two_pi * hf, two_pi * kf, two_pi * l_col / BOX_Z
@@ -238,11 +241,14 @@
     pl.semaphore_wait(barrier, devices - 1)
     each(devices, lambda o: mail_copy(o).start())
     cz, sz = turns(l_col, coords[2:3])
-    v1h, v1l = split2(q * jnp.where(is_re, cz, sz))
-    v2h, v2l = split2(q * jnp.where(is_re, -sz, cz))
+    wide = 128
+    blank = jnp.zeros((wide - L_ROWS, slots), F32)
+    v1h, v1l = split2(jnp.concatenate([q * jnp.where(is_re, cz, sz), blank]))
+    v2h, v2l = split2(jnp.concatenate([q * jnp.where(is_re, -sz, cz), blank]))
     uch, ush, ucl, usl = (table[pl.ds(i * PAIRS, PAIRS), :slots] for i in range(4))
-    total = mm(v1l, uch, NT) + mm(v1h, ucl, NT) + mm(v2l, ush, NT) + mm(v2h, usl, NT)
-    total = total + (mm(v1h, uch, NT) + mm(v2h, ush, NT))
+    low = mm(ucl, v1h, NT) + mm(usl, v2h, NT)
+    both = mm(uch, jnp.concatenate([v1h, v1l]), NT) + mm(ush, jnp.concatenate([v2h, v2l]), NT)
+    total = (both[:, :wide] + (both[:, wide:] + low)).T
     for t in range(tile_count):
         if t < TILES:
             i, j = t // P_TILES, t % P_TILES
@@ -311,7 +317,9 @@
     fz = jnp.sum(x[:L_ROWS] * (two_pi * l_col / BOX_Z), axis=0, keepdims=True)
     fx = two_pi * jnp.sum(x[L_ROWS : 2 * L_ROWS], axis=0, keepdims=True)
     fy = two_pi * jnp.sum(x[2 * L_ROWS :], axis=0, keepdims=True)
-    forces[...] = scale * charge * jnp.concatenate([fx, fy, fz])
+    force = scale * charge * jnp.concatenate([fx, fy, fz])
+    forces[:, :slots] = jnp.where(live, force[:, :slots], 0.0)
+    forces[:, slots:] = force[:, slots:]
 
     each(devices, lambda o: mail_copy(o).wait_send())
     sib_copy().wait_send()
@@ -321,10 +329,9 @@
     each(chips, lambda o: pass_on(o).wait_send())
 
 
-def deliver(counts, forces, slot_forces, atom_forces):
+def deliver(forces, slot_forces, atom_forces):
     slots = slot_forces.shape[1]
-    live = iota((1, slots), 1) < counts[0]
-    slot_forces[...] = jnp.where(live, forces[:, :slots], 0.0)
+    slot_forces[...] = forces[:, :slots]
     atom_forces[...] = forces[:, slots:]
 
 
@@ -368,9 +375,9 @@
     return pl.pallas_call(
         deliver,
         out_shape=[shape((3, slots), F32), shape((3, atoms), F32)],
-        in_specs=[SMEM, VMEM],
+        in_specs=[VMEM],
         out_specs=[VMEM] * 2,
-    )(counts, forces)
+    )(forces)
 
 
 def solution(mesh):

time: 27.4 us -> 27.5 us (level)
  no operation moved by 1% of the time
where the time goes in v4:
time: 27.5 us; the launch traced here: 27.3 us
  Pallas kernels  26 us (95%)
  between operations  1.28 us (5%)
    pallas_call x1, Pallas kernels, body(): pl.pallas_call(functools.partial(kernel, blks, rows, cap, scale), out_sha...  24.6 us
    pallas_call x1, Pallas kernels, body(): pl.pallas_call(deliver, out_shape=[shape((3, slots), F32), shape((3, atom...  1.33 us

profile of v4, /device:TPU:1, one launch (start us, length us, event | category | flops | bytes accessed | tf_op | source)
XLA Modules:
  0.0 27.3 jit_solution(17380343392545189187)
XLA Ops:
  1.3 24.6 %shard_map.77.forces = f32[3,1280]{1,0:T(4,128)} custom-call(f32[3,768]{1,0:T(4,128)} %coords.1, f32[768]{0:T(1024)} %charges.1, s32[1]{0:T(128)S(6)} %copy.8.counts, s32[768]{0:T(1024)} %send_slot.1, s32[512]{0:T(512)} %recv_index.1, s32[3,6144]{1,0:T(4,128)} %wave.1), custom_call_target="tpu_custom_call" | custom-call | tf_op jit(solution)/shard_map/pallas_call | solution.py:354
  25.9 1.3 %shard_map.78 = (f32[3,768]{1,0:T(4,128)}, f32[3,512]{1,0:T(4,128)}) custom-call(f32[3,1280]{1,0:T(4,128)} %shard_map.77.forces), custom_call_target="tpu_custom_call" | custom-call | tf_op jit(solution)/shard_map/pallas_call | solution.py:375

commit v5 on v4

--- a/solution.py
+++ b/solution.py
@@ -262,6 +262,16 @@
 
     each(devices, lambda o: mail_copy(o).wait_recv())
     got_mail[0] = mail[me]
+    m_own = got_mail[0, :share]
+    for o in range(1, devices):
+        m_own = m_own + got_mail[o, :share]
+    each(chips, lambda o: sums_copy(o).wait_recv())
+    got_t[0] = half_sums[pl.ds(chip * share, share)]
+    piece = jnp.sum(got_t[...], axis=0) * jnp.concatenate([m_own, m_own], axis=1)
+    own[...] = piece
+    each(chips, lambda o: grid_copy(o).start())
+    pass_on(0).start()
+    grid[pl.ds(mine + chip * share, share)] = piece
     arrived = []
     for t in range(devices // per_tile):
         tile = jnp.zeros((4, 128), F32)
@@ -273,18 +283,7 @@
     index = recv_index[...].reshape(1, atoms)
     picks = jnp.where(index == iota((came.shape[1], atoms), 0), 1.0, 0.0).astype(BF16)
     ions = sum(mm(term, picks, NN) for term in split3(came))
-    m_own = got_mail[0, :share]
-    for o in range(1, devices):
-        m_own = m_own + got_mail[o, :share]
-
     fill_pairs(ions[0:1], ions[1:2], table, slots)
-    each(chips, lambda o: sums_copy(o).wait_recv())
-    got_t[0] = half_sums[pl.ds(chip * share, share)]
-    piece = jnp.sum(got_t[...], axis=0) * jnp.concatenate([m_own, m_own], axis=1)
-    own[...] = piece
-    each(chips, lambda o: grid_copy(o).start())
-    pass_on(0).start()
-    grid[pl.ds(mine + chip * share, share)] = piece
     cz2, sz2 = turns(l_col, ions[2:3])
     vf = jnp.where(is_re, jnp.concatenate([sz, sz2], axis=1), jnp.concatenate([cz, cz2], axis=1))
     charge = jnp.concatenate([q, ions[3:4]], axis=1)

time: 27.5 us -> 27.5 us (level)
  no operation moved by 1% of the time
where the time goes in v5:
time: 27.5 us; the launch traced here: 27.3 us
  Pallas kernels  26 us (95%)
  between operations  1.28 us (5%)
    pallas_call x1, Pallas kernels, body(): pl.pallas_call(functools.partial(kernel, blks, rows, cap, scale), out_sha...  24.6 us
    pallas_call x1, Pallas kernels, body(): pl.pallas_call(deliver, out_shape=[shape((3, slots), F32), shape((3, atom...  1.33 us

profile of v5, /device:TPU:1, one launch (start us, length us, event | category | flops | bytes accessed | tf_op | source)
XLA Modules:
  0.0 27.3 jit_solution(9259339866289608004)
XLA Ops:
  1.3 24.6 %shard_map.77.forces = f32[3,1280]{1,0:T(4,128)} custom-call(f32[3,768]{1,0:T(4,128)} %coords.1, f32[768]{0:T(1024)} %charges.1, s32[1]{0:T(128)S(6)} %copy.8.counts, s32[768]{0:T(1024)} %send_slot.1, s32[512]{0:T(512)} %recv_index.1, s32[3,6144]{1,0:T(4,128)} %wave.1), custom_call_target="tpu_custom_call" | custom-call | tf_op jit(solution)/shard_map/pallas_call | solution.py:353
  25.9 1.3 %shard_map.78 = (f32[3,768]{1,0:T(4,128)}, f32[3,512]{1,0:T(4,128)}) custom-call(f32[3,1280]{1,0:T(4,128)} %shard_map.77.forces), custom_call_target="tpu_custom_call" | custom-call | tf_op jit(solution)/shard_map/pallas_call | solution.py:374
